TPU v7x, 256 devices: a whole 4x4x8 slice. The times are simulated.
256 devices in a mesh: seq: 8 (over y, core), mp: 32 (over z, x).
Axes of the slice: x: 4, y: 4, z: 8, core: 2. Of those that a mesh axis runs over, the one named last changes fastest.
Arguments:
- tokens: bfloat16 [4096, 8192], P('seq', 'mp')
- norm_gain: float32 [8192], replicated, may hold values from 0.1 to 1.9
- query_weight: bfloat16 [8192, 8192], P(None, 'mp')
- pair_weight: bfloat16 [8192, 2048], P(None, 'mp')
- ancestors: int32 [32, 5], replicated, may hold values from -1 to 30, as said below
- out_weight: bfloat16 [8192, 8192], P('mp'), may hold values from -0.125 to 0.125
Outputs:
- mixed: bfloat16 [4096, 8192], P('seq', 'mp')
Inputs may be any that keep to these rules, and one draw needn't show every extreme that they name: `ancestors`: one tree of 32 blocks starts with 4 prompt blocks; a prompt block lists the earlier prompt blocks. Every later block is a response block: it lists a leading run of 1 to 4 prompt blocks in its first entries and, in its last entry, either -1 or its parent, an earlier response block, whose leading run of prompt blocks it shares. The first response block lists all prompt blocks and no parent; the last block's parent is the block before it. Unused entries are -1; a block never lists itself.
All inputs are finite; a program needn't handle non-finite values.
Results may differ from a plain program's by a relative error of at most 0.0095.
Values may be sent and summed in bfloat16 or wider, within the bound.
A program may use at most 128 MiB of HBM per device.

v0:
```python
import jax
import jax.numpy as jnp
from jax import lax
from jax.sharding import PartitionSpec as P

HQ = 64
KVH = 8
HD = 128
BLK = 128


epsilon = 1e-05
neg_large = -1e30


def local(tokens, norm_gain, query_weight, pair_weight, ancestors, out_weight):
    tok_rows = tokens.shape[0]
    heads_here = query_weight.shape[1] // HD
    whole = lax.all_gather(tokens, "mp", axis=1, tiled=True)
    tok_float = whole.astype(jnp.float32)
    mean_square = jnp.mean(tok_float * tok_float, axis=1, keepdims=True)
    normed = (tok_float * lax.rsqrt(mean_square + epsilon) * norm_gain).astype(jnp.bfloat16)
    query_full = jnp.dot(normed, query_weight, preferred_element_type=jnp.float32)
    pair_full = jnp.dot(normed, pair_weight, preferred_element_type=jnp.float32)
    queries = query_full.astype(jnp.bfloat16).reshape(tok_rows, heads_here, HD)
    pair_local = pair_full.astype(jnp.bfloat16)
    pair_columns = lax.all_gather(pair_local, "mp", axis=1, tiled=True)
    kv_group = lax.axis_index("mp") * heads_here // (HQ // KVH)
    own_keys = lax.dynamic_slice_in_dim(pair_columns, kv_group * HD, HD, 1)
    own_values = lax.dynamic_slice_in_dim(pair_columns, KVH * HD + kv_group * HD, HD, 1)
    own_pairs = jnp.concatenate([own_keys, own_values], axis=1)
    blocks_here = tok_rows // BLK
    first_block = lax.axis_index("seq") * blocks_here
    own_lists = lax.dynamic_slice_in_dim(ancestors, first_block, blocks_here, 0)
    query_ids = first_block + jnp.arange(blocks_here, dtype=jnp.int32)
    score_scale = HD ** (-0.5)
    causal_ok = jnp.arange(BLK)[:, None] >= jnp.arange(BLK)[None, :]
    panel_x = lax.all_gather(own_pairs, "seq", axis=0, tiled=True)
    run_max = jnp.full((tok_rows, heads_here), neg_large, jnp.float32)
    panel_rows = panel_x.shape[0]
    key_ids = jnp.arange(panel_rows // BLK, dtype=jnp.int32)
    list_hit = jnp.any(own_lists[:, :, None] == key_ids[None, None, :], axis=1)
    self_hit = query_ids[:, None] == key_ids[None, :]
    allowed = list_hit[:, None, :, None] | self_hit[:, None, :, None] & causal_ok[None, :, None, :]
    allowed = allowed.reshape(tok_rows, panel_rows)[:, None, :]
    scores = (
        jnp.einsum("thd,ud->thu", queries, panel_x[:, :HD], preferred_element_type=jnp.float32)
        * score_scale
    )
    masked_scores = jnp.where(allowed, scores, neg_large)
    new_max = jnp.maximum(run_max, jnp.max(masked_scores, axis=2))
    weights = jnp.where(allowed, jnp.exp(masked_scores - new_max[:, :, None]), 0.0)
    new_sum = jnp.sum(weights, axis=2)
    new_acc = jnp.einsum(
        "thu,ud->thd",
        weights.astype(jnp.bfloat16),
        panel_x[:, HD:],
        preferred_element_type=jnp.float32,
    )
    attended = (
        (new_acc / new_sum[:, :, None]).astype(jnp.bfloat16).reshape(tok_rows, heads_here * HD)
    )
    head_terms = jnp.dot(attended, out_weight, preferred_element_type=jnp.float32)
    return lax.psum_scatter(head_terms, "mp", scatter_dimension=1, tiled=True).astype(jnp.bfloat16)


def solution(mesh):
    return jax.shard_map(
        local,
        mesh=mesh,
        in_specs=(P("seq", "mp"), P(), P(None, "mp"), P(None, "mp"), P(), P("mp", None)),
        out_specs=P("seq", "mp"),
        check_vma=False,
    )
```

profile of v0, /device:TPU:8, one launch (start us, length us, event | category | flops | bytes accessed | tf_op | source)
XLA Modules:
  0.0 509.7 jit_solution(2918348724741647176)
XLA Ops:
  6.5 0.0 copy-start
  6.5 0.0 copy-start.3
  6.5 0.0 copy-start.2
  6.5 0.0 all-gather.4.cloned.1.call-start
  6.5 0.7 all-gather.4.cloned.1.call-update
  7.3 0.0 all-gather.6.cloned.1.call-start
  7.3 109.1 %all-gather.4.cloned.1.call-done = bf16[512,8192]{1,0:T(8,128)(2,1)} async-done(((bf16[512,256]{1,0:T(8,128)(2,1)}), bf16[512,8192]{1,0:T(8,128)(2,1)}) %all-gather.4.cloned.1.call-update) | async-done | bytes 8388624 | tf_op jit(solution)/shard_map/all_gather | solution.py:19
  116.4 5.1 %fusion = f32[512]{0:T(512)S(1)} fusion(bf16[512,8192]{1,0:T(8,128)(2,1)} %all-gather.4.cloned.1.call-done), kind=kLoop, calls=%fused_computation.2 | loop fusion | flops 12582400 | bytes 8390656 | tf_op jit(solution)/shard_map/reduce_sum | solution.py:21
  121.5 0.0 copy-done
  121.5 6.7 %fusion.16 = bf16[512,64]{0,1:T(8,128)(2,1)} fusion(bf16[8192,64]{0,1:T(8,128)(2,1)S(1)} %copy-done, bf16[512,8192]{1,0:T(8,128)(2,1)} %all-gather.4.cloned.1.call-done, f32[8192]{0:T(1024)} %param.7, f32[512]{0:T(512)S(1)} %add_rsqrt_fusion), kind=kOutput, calls=%fused_computation.17 | convolution fusion | flops 553680896 | bytes 9537536 | tf_op jit(solution)/shard_map/dot_general | solution.py:24
  128.2 0.0 all-gather.6.cloned.1.call-update
  128.3 0.0 all-gather.8.cloned.1.call-start
  128.3 75.6 %all-gather.6.cloned.1.call-done = bf16[512,2048]{0,1:T(8,128)(2,1)} async-done(((bf16[512,64]{0,1:T(8,128)(2,1)}), bf16[512,2048]{0,1:T(8,128)(2,1)}) %all-gather.6.cloned.1.call-update) | async-done | bytes 2097168 | tf_op jit(solution)/shard_map/all_gather | solution.py:27
  203.9 1.0 constant_dynamic-slice_fusion.1
  204.9 0.7 pad_maximum_fusion
  205.6 0.0 all-gather.8.cloned.1.call-update
  205.6 0.0 reduce-scatter.2.cloned.1.call-start
  205.7 0.0 copy-done.2
  205.7 0.1 constant_dynamic-slice_fusion.2
  205.8 0.1 fusion.26
  205.9 0.1 iota_compare_fusion.2
  206.0 1.4 and_or_fusion
  207.3 1.6 copy.17
  208.9 0.0 copy-done.3
  208.9 7.4 %fusion.13 = bf16[512,256]{0,1:T(8,128)(2,1)S(1)} fusion(bf16[8192,256]{1,0:T(8,128)(2,1)} %param.8, bf16[512,8192]{1,0:T(8,128)(2,1)} %all-gather.4.cloned.1.call-done, f32[8192]{0:T(1024)S(1)} %copy-done.3, f32[512]{0:T(512)S(1)} %add_rsqrt_fusion), kind=kOutput, calls=%fused_computation.16 | convolution fusion | flops 2164391936 | bytes 12879872 | tf_op jit(solution)/shard_map/dot_general | solution.py:23
  216.4 13.4 %all-gather.8.cloned.1.call-done = bf16[4096,256]{0,1:T(8,128)(2,1)} async-done(((bf16[512,256]{0,1:T(8,128)(2,1)}), bf16[4096,256]{0,1:T(8,128)(2,1)}) %all-gather.8.cloned.1.call-update) | async-done | bytes 2097168 | tf_op jit(solution)/shard_map/all_gather | solution.py:38
  229.8 4.9 fusion.3
  234.7 5.3 %fusion.4 = f32[512,2]{0,1:T(2,128)S(1)} fusion(f32[512,2,4096]{2,0,1:T(8,128)S(1)} %get-tuple-element.8, f32[512,2]{0,1:T(2,128)S(1)} %broadcast_maximum_fusion, pred[512,4096]{1,0:T(8,128)(4,1)S(1)} %bitcast.25), kind=kLoop, calls=%fused_computation.8 | loop fusion | flops 20970496 | bytes 18882560 | tf_op jit(solution)/shard_map/reduce_sum | solution.py:53
  240.0 0.0 copy-start.1
  240.0 6.9 %fusion.23 = bf16[512,2,128]{0,2,1:T(8,128)(2,1)S(1)} fusion(bf16[4096,256]{0,1:T(8,128)(2,1)} %all-gather.8.cloned.1.call-done, f32[512,2,4096]{2,0,1:T(8,128)S(1)} %get-tuple-element.8, f32[512,2]{0,1:T(2,128)S(1)} %broadcast_maximum_fusion, pred[512,4096]{1,0:T(8,128)(4,1)S(1)} %bitcast.26, f32[512,2]{0,1:T(2,128)S(1)} %fusion.4), kind=kOutput, calls=%fused_computation.22 | convolution fusion | flops 1094975488 | bytes 20193280 | tf_op jit(solution)/shard_map/thu,ud->thd/dot_general | solution.py:54
  246.9 0.0 copy-done.1
  246.9 8.1 %fusion.30 = f32[512,8192]{1,0:T(8,128)} fusion(bf16[512,256]{0,1:T(8,128)(2,1)S(1)} %bitcast.28, bf16[256,8192]{1,0:T(8,128)(2,1)S(1)} %copy-done.1), kind=kOutput, calls=%fused_computation.37 | convolution fusion | flops 2147483648 | bytes 21233664 | tf_op jit(solution)/shard_map/dot_general | solution.py:63
  255.0 0.0 reduce-scatter.2.cloned.1.call-update
  255.1 246.4 %reduce-scatter.2.cloned.1.call-done = f32[512,256]{1,0:T(8,128)} async-done(((f32[512,8192]{1,0:T(8,128)}), f32[512,256]{1,0:T(8,128)}) %reduce-scatter.2.cloned.1.call-update) | async-done | bytes 524304 | tf_op jit(solution)/shard_map/reduce_scatter | solution.py:64
  501.4 1.8 convert_element_type.27
  (4 shorter events, 0.0 us)
Async XLA Ops:
  6.5 115.0 %copy-start = (bf16[8192,64]{0,1:T(8,128)(2,1)S(1)}, bf16[8192,64]{0,1:T(8,128)(2,1)}, u32[]{:S(2)}) copy-start(bf16[8192,64]{0,1:T(8,128)(2,1)} %param.9) | copy-start | bytes 3145732
  6.5 202.4 %copy-start.3 = (f32[8192]{0:T(1024)S(1)}, f32[8192]{0:T(1024)}, u32[]{:S(2)}) copy-start(f32[8192]{0:T(1024)} %param.7) | copy-start | bytes 98308
  6.5 199.2 %copy-start.2 = (s32[32,5]{0,1:T(8,128)S(1)}, s32[32,5]{0,1:T(8,128)}, u32[]{:S(2)}) copy-start(s32[32,5]{0,1:T(8,128)} %param.10) | copy-start | bytes 1924
  6.5 109.8 %all-gather.4.cloned.1.call-start = ((), (), s32[]{:S(2)}) async-start(), calls=%async_computation.1 | async-start | bytes 8650752 | tf_op jit(solution)/shard_map/all_gather | solution.py:19
  7.3 196.6 %all-gather.6.cloned.1.call-start = ((), (), s32[]{:S(2)}) async-start(), calls=%async_computation.2 | async-start | bytes 2162688 | tf_op jit(solution)/shard_map/all_gather | solution.py:27
  128.3 101.6 %all-gather.8.cloned.1.call-start = ((), (), s32[]{:S(2)}) async-start(), calls=%async_computation.3 | async-start | bytes 2359296 | tf_op jit(solution)/shard_map/all_gather | solution.py:38
  205.6 295.8 %reduce-scatter.2.cloned.1.call-start = ((), (), s32[]{:S(2)}) async-start(), calls=%async_computation.4 | async-start | bytes 17301504 | tf_op jit(solution)/shard_map/reduce_scatter | solution.py:64
  240.0 6.9 %copy-start.1 = (bf16[256,8192]{1,0:T(8,128)(2,1)S(1)}, bf16[256,8192]{1,0:T(8,128)(2,1)}, u32[]{:S(2)}) copy-start(bf16[256,8192]{1,0:T(8,128)(2,1)} %param.11) | copy-start | bytes 12582916
Sparse Core Ops, SparseCore 0:
  9.8 106.4 all-gather.3
  128.4 75.4 all-gather.5
  205.7 24.0 all-gather.7
  255.2 246.1 reduce-scatter.1
where the time goes:
time: 510 us
  waiting for transfers between devices  445 us (87%)
  matrix products  34.1 us (7%)
  other arithmetic  14.5 us (3%)
  between operations  13.3 us (3%)
    reduce_scatter x1, waiting for transfers between devices, local(): lax.psum_scatter(head_terms, 'mp', scatter_dimension=1, tiled=True)  246 us
    all_gather x1, waiting for transfers between devices, local(): whole = lax.all_gather(tokens, 'mp', axis=1, tiled=True)  109 us
    all_gather x1, waiting for transfers between devices, local(): pair_columns = lax.all_gather(pair_local, 'mp', axis=1, tiled=True)  75.6 us
    all_gather x1, waiting for transfers between devices, local(): panel_x = lax.all_gather(own_pairs, 'seq', axis=0, tiled=True)  13.4 us
  transfers between devices with their start and end apart: 4, of which 4 were waited for; matrix products, arithmetic and copies ran while one was open for 2% of the time, Pallas kernels for 0%

commit v1 on v0

v1 whole, which is shorter than its diff:
```python
import functools

import jax
import jax.numpy as jnp
from jax import lax
from jax.experimental import pallas as pl
from jax.experimental.pallas import tpu as pltpu
from jax.sharding import PartitionSpec as P

MESH = pl.DeviceIdType.MESH
HD = 128
BLK = 128
NX, NY, NZ = 4, 4, 8
FEATURES = 8192
EPS = 1e-05
NEG = -1e30
F32 = jnp.float32
BF16 = jnp.bfloat16


def nt_dot(a, b):
    return lax.dot_general(a, b, (((1,), (1,)), ((), ())), preferred_element_type=F32)


def kernel(
    anc, gain, tok, wq, pwt, wo, out,
    xg, xn, rcol, ssx, ssz, wb, wob, kvs, kvr, kvown, kvtab, qs, qr, qown, qb, attb, rsend, rrecv,
    local_sem, x_s, x_r, ssx_s, ssx_r, ssz_s, ssz_r,
    w_s, w_r, p_s, p_r, wy_s, wy_r, wc_s, wc_r,
    o_s, o_r, oy_s, oy_r, oc_s, oc_r,
    kv_s, kv_r, ka_s, ka_r, ky_s, ky_r, kc_s, kc_r, q_s, q_r, at_s, at_r, rs_s, rs_r,
):
    s = lax.axis_index("seq")
    m = lax.axis_index("mp")
    y, c = s // 2, s % 2
    z, x = m // NX, m % NX

    def at_x(d):
        return (s, z * NX + (x + d) % NX)

    def at_z(k):
        return (s, ((z + k + NZ) % NZ) * NX + x)

    def at_y(e):
        return (((y + e) % NY) * 2 + c, m)

    sibling = (y * 2 + 1 - c, m)

    def lane_strip(e):
        return ((y + e) % NY) * 2 + c

    def far_strip(e):
        return ((y + e) % NY) * 2 + 1 - c

    def remote(src, dst, ss, rs, dev):
        return pltpu.make_async_remote_copy(
            src_ref=src, dst_ref=dst, send_sem=ss, recv_sem=rs, device_id=dev, device_id_type=MESH
        )

    pair_q = (m // 16) * 2 + m % 2
    pair_z = (m // 2) % NZ

    barrier = pltpu.get_barrier_semaphore()
    peers = [at_x(d) for d in (1, 2, 3)] + [at_z(k) for k in range(1, NZ)] + [at_y(e) for e in (1, 2, 3)] + [sibling]
    for dev in peers:
        pl.semaphore_signal(barrier, inc=1, device_id=dev, device_id_type=MESH)
    for source in (2 * z, 2 * z + 1, 16 + 2 * z, 17 + 2 * z):

        @pl.when(source != m)
        def _():
            pl.semaphore_signal(barrier, inc=1, device_id=(s, source), device_id_type=MESH)

    own_x = pltpu.make_async_copy(tok, xg.at[z], local_sem.at[0])
    own_x.start()
    own_w = pltpu.make_async_copy(wq.at[:, x], wb.at[0], local_sem.at[1])
    own_w.start()
    pl.semaphore_wait(barrier, len(peers) + jnp.where(pair_z == z, 3, 4))

    def rows(b):
        return pl.ds(b * BLK, BLK)

    def x_copy(way, hop, b):
        step = 1 if way == 0 else -1
        shard = (z - step * hop + NZ) % NZ
        src = tok.at[rows(b)] if hop == 0 else xg.at[shard, rows(b)]
        return remote(src, xg.at[shard, rows(b)], x_s.at[way, hop, b], x_r.at[way, hop, b], at_z(step))

    def x_arrival(way, hop, b):
        step = 1 if way == 0 else -1
        shard = (z - step * (hop + 1) + NZ) % NZ
        ref = xg.at[shard, rows(b)]
        return remote(ref, ref, x_s.at[way, hop, b], x_r.at[way, hop, b], at_z(step))

    def x_used(way, hop, b):
        return hop < 3 or (b < 2) == (way == 0)

    for b in range(4):
        for way in range(2):
            x_copy(way, 0, b).start()

    def w_copy(i, d):
        strip = lane_strip(2 * i)
        return remote(wq.at[strip, (x + d) % NX], wb.at[4 - d, strip], w_s.at[i, d - 1], w_r.at[i, 3 - d], at_x(d))

    def p_copy(i, x2):
        strip = lane_strip(2 * i)
        src = pwt.at[:, pl.ds(pl.multiple_of((strip * NX + x2) * 256, 256), 256)]
        dst = wb.at[4, strip, pl.ds(pl.multiple_of(pair_q * 64, 64), 64), :]
        return remote(src, dst, p_s.at[i, x2], p_r.at[i, pair_q], (s, pair_z * NX + x2)), src, dst

    def p_self(x2):
        return jnp.logical_and(pair_z == z, x == x2)

    def p_start(i):
        for x2 in range(NX):
            cp, src, dst = p_copy(i, x2)

            @pl.when(p_self(x2))
            def _():
                pltpu.make_async_copy(src, dst, p_r.at[i, pair_q]).start()

            @pl.when(jnp.logical_not(p_self(x2)))
            def _():
                cp.start()

    for i in range(2):
        for d in (1, 3, 2):
            w_copy(i, d).start()
        p_start(i)

    own_x.wait()
    row_id = lax.broadcasted_iota(jnp.int32, (8, BLK), 0)
    part = jnp.zeros((8, BLK), F32)
    for b in range(4):
        xf = xg[z, b * BLK : (b + 1) * BLK, :].astype(F32)
        sums = jnp.broadcast_to(jnp.sum(xf * xf, axis=1, keepdims=True), (BLK, BLK)).T
        part = jnp.where(row_id == b, sums[:8], part)
    ssx[0] = part

    def ssx_copy(d):
        return remote(ssx.at[0], ssx.at[4 - d], ssx_s.at[d - 1], ssx_r.at[3 - d], at_x(d))

    def ssz_copy(k):
        return remote(ssz.at[0], ssz.at[NZ - k], ssz_s.at[k - 1], ssz_r.at[NZ - 1 - k], at_z(k))

    for d in (1, 3, 2):
        ssx_copy(d).start()

    def x_forward(hop):
        for b in range(4):
            for way in range(2):
                if x_used(way, hop, b):
                    x_arrival(way, hop, b).wait_recv()
                    if hop < 3 and x_used(way, hop + 1, b):
                        x_copy(way, hop + 1, b).start()

    x_forward(0)
    for d in (1, 2, 3):
        ssx_copy(d).wait_recv()
    ssz[0] = ssx[0] + ssx[1] + ssx[2] + ssx[3]
    for k in (1, 7, 2, 6, 3, 5, 4):
        ssz_copy(k).start()

    def wy_copy(e):
        src = wb.at[pl.ds(1, 4), s]
        return remote(src, src, wy_s.at[e // 2], wy_r.at[(3 - e) // 2], at_y(e))

    def wy_arrival(e):
        ref = wb.at[pl.ds(1, 4), lane_strip(e)]
        return remote(ref, ref, wy_s.at[e // 2], wy_r.at[e // 2], at_y(e))

    def wc_copy(e):
        src = wb.at[pl.ds(1, 4), lane_strip(e)]
        return remote(src, src, wc_s.at[e], wc_r.at[e], sibling)

    def wc_arrival(e):
        ref = wb.at[pl.ds(1, 4), far_strip(e)]
        return remote(ref, ref, wc_s.at[e], wc_r.at[e], sibling)

    def w_arrive(i):
        strip = lane_strip(2 * i)
        for d in (1, 2, 3):
            ref = wb.at[d, strip]
            remote(ref, ref, w_s.at[i, d - 1], w_r.at[i, d - 1], at_x(d)).wait_recv()
        for q in range(4):
            ref = wb.at[4, strip, pl.ds(q * 64, 64), :]
            remote(ref, ref, p_s.at[i, q], p_r.at[i, q], sibling).wait_recv()

    w_arrive(0)
    wy_copy(1).start()
    wy_copy(3).start()
    wc_copy(0).start()
    x_forward(1)

    for k in range(1, NZ):
        ssz_copy(k).wait_recv()
    total = ssz[0]
    for k in range(1, NZ):
        total = total + ssz[k]
    scale = lax.rsqrt(total * (1.0 / FEATURES) + EPS)
    for b in range(4):
        rcol[b] = jnp.broadcast_to(scale[b : b + 1, :], (BLK, BLK)).T

    def normalise(shard):
        g = gain[pl.ds(shard * NX + x, 1), :]

        def one(b, carry):
            at = pl.ds(pl.multiple_of(b * BLK, BLK), BLK)
            r = rcol[b]
            v = xg[shard, at, :].astype(F32) * jnp.concatenate([r, r], axis=1) * g
            xn[at, pl.ds(pl.multiple_of(shard * 256, 256), 256)] = v.astype(BF16)
            return carry

        lax.fori_loop(0, 4, one, 0)

    normalise(z)
    normalise((z + 1) % NZ)
    normalise((z + 7) % NZ)
    w_arrive(1)
    wc_copy(2).start()

    def wo_block(strip, x2):
        return wo.at[:, pl.ds(pl.multiple_of((strip * NX + x2) * 256, 256), 256)]

    own_wo = [pltpu.make_async_copy(wo_block(k, x), wob.at[0, k], local_sem.at[2 + k]) for k in range(NZ)]
    for cp in own_wo:
        cp.start()

    def o_copy(i, d):
        strip = lane_strip(2 * i)
        return remote(wo_block(strip, (x + d) % NX), wob.at[4 - d, strip], o_s.at[i, d - 1], o_r.at[i, 3 - d], at_x(d))

    def oy_copy(e):
        src = wob.at[pl.ds(1, 3), s]
        return remote(src, src, oy_s.at[e // 2], oy_r.at[(3 - e) // 2], at_y(e))

    def oy_arrival(e):
        ref = wob.at[pl.ds(1, 3), lane_strip(e)]
        return remote(ref, ref, oy_s.at[e // 2], oy_r.at[e // 2], at_y(e))

    def oc_copy(e):
        src = wob.at[pl.ds(1, 3), lane_strip(e)]
        return remote(src, src, oc_s.at[e], oc_r.at[e], sibling)

    def oc_arrival(e):
        ref = wob.at[pl.ds(1, 3), far_strip(e)]
        return remote(ref, ref, oc_s.at[e], oc_r.at[e], sibling)

    def o_arrive(i):
        strip = lane_strip(2 * i)
        for d in (1, 2, 3):
            ref = wob.at[d, strip]
            remote(ref, ref, o_s.at[i, d - 1], o_r.at[i, d - 1], at_x(d)).wait_recv()

    for i in range(2):
        for d in (1, 3, 2):
            o_copy(i, d).start()

    x_forward(2)
    normalise((z + 2) % NZ)
    normalise((z + 6) % NZ)
    for e in (1, 3):
        wy_arrival(e).wait_recv()
        wc_copy(e).start()
    normalise((z + 3) % NZ)
    normalise((z + 5) % NZ)
    x_forward(3)
    normalise((z + 4) % NZ)
    for e in range(4):
        wc_arrival(e).wait_recv()
    own_w.wait()

    acc = nt_dot(xn[:, :256], wb[4, 0])
    for k in range(1, NZ):
        acc = acc + nt_dot(xn[:, k * 256 : (k + 1) * 256], wb[4, k])
    kvown[...] = acc.reshape(4, BLK, 256)
    kvs[...] = acc.astype(BF16).reshape(4, BLK, 256)

    def kv_copy(d):
        return remote(kvs.at[(x + d) % NX], kvr.at[3 - d], kv_s.at[d - 1], kv_r.at[3 - d], at_x(d))

    for d in (1, 3, 2):
        kv_copy(d).start()

    def q_copy(xa, d):
        return remote(qs.at[xa, (x + d) % NX], qr.at[3 - d, xa], q_s.at[xa, d - 1], q_r.at[xa, 3 - d], at_x(d))

    def q_part(d, carry):
        xa = (x + d) % NX
        a = jnp.dot(xn[...], wb[d].reshape(2048, 256), preferred_element_type=F32).reshape(4, BLK, 256)
        qs[xa] = a.astype(BF16)
        qown[xa] = a
        for e in (1, 3, 2):
            q_copy(xa, e).start()
        return carry

    lax.fori_loop(0, 4, q_part, 0)

    block = s * NX + x
    for d in (1, 2, 3):
        kv_copy(d).wait_recv()
    mine = kvown[x] + kvr[0].astype(F32) + kvr[1].astype(F32) + kvr[2].astype(F32)
    kvtab[block] = mine.astype(BF16)

    def ka_copy(d):
        return remote(kvtab.at[block], kvtab.at[block], ka_s.at[d - 1], ka_r.at[3 - d], at_x(d))

    def ka_arrival(d):
        ref = kvtab.at[s * NX + (x + d) % NX]
        return remote(ref, ref, ka_s.at[d - 1], ka_r.at[d - 1], at_x(d))

    for d in (1, 3, 2):
        ka_copy(d).start()
    o_arrive(0)
    oy_copy(1).start()
    oy_copy(3).start()
    oc_copy(0).start()

    def group(strip):
        return kvtab.at[pl.ds(strip * NX, NX)]

    def ky_copy(e):
        return remote(group(s), group(s), ky_s.at[e - 1], ky_r.at[3 - e], at_y(e))

    def ky_arrival(e):
        ref = group(lane_strip(e))
        return remote(ref, ref, ky_s.at[e - 1], ky_r.at[e - 1], at_y(e))

    def kc_copy(e):
        ref = group(lane_strip(e))
        return remote(ref, ref, kc_s.at[e], kc_r.at[e], sibling)

    def kc_arrival(e):
        ref = group(far_strip(e))
        return remote(ref, ref, kc_s.at[e], kc_r.at[e], sibling)

    for d in (1, 3, 2):
        ka_arrival(d).wait_recv()
    for e in (1, 3, 2):
        ky_copy(e).start()
    kc_copy(0).start()

    o_arrive(1)
    oc_copy(2).start()

    for xa in range(NX):
        for d in (1, 2, 3):
            q_copy(xa, d).wait_recv()
        v = qown[xa, x] + qr[0, xa].astype(F32) + qr[1, xa].astype(F32) + qr[2, xa].astype(F32)
        qb[xa] = v.astype(BF16)

    for e in (1, 3):
        oy_arrival(e).wait_recv()
        oc_copy(e).start()
    for e in (1, 3, 2):
        ky_arrival(e).wait_recv()
        kc_copy(e).start()
    for e in range(4):
        kc_arrival(e).wait_recv()

    listed = [anc[block, j] for j in range(5)]
    tables = [kvtab[jnp.maximum(i, 0)] for i in listed] + [kvtab[block]]
    causal = lax.broadcasted_iota(jnp.int32, (BLK, BLK), 0) >= lax.broadcasted_iota(jnp.int32, (BLK, BLK), 1)
    causal = jnp.concatenate([causal, causal], axis=0)
    for xa in range(NX):
        q2 = jnp.concatenate([qb[xa, :, :HD], qb[xa, :, HD:]], axis=0)
        masks, scores = [], []
        for j in range(6):
            sc = nt_dot(q2, tables[j][:, :HD]) * HD**-0.5
            ok = causal if j == 5 else jnp.broadcast_to(listed[j], (2 * BLK, BLK)) >= 0
            masks.append(ok)
            scores.append(jnp.where(ok, sc, NEG))
        top = functools.reduce(jnp.maximum, scores)
        top = jnp.max(top, axis=1, keepdims=True)
        weights = [jnp.where(ok, jnp.exp(sc - top), 0.0) for ok, sc in zip(masks, scores)]
        total = jnp.sum(functools.reduce(jnp.add, weights), axis=1, keepdims=True)
        got = jnp.zeros((2 * BLK, HD), F32)
        for j in range(6):
            got = got + jnp.dot(weights[j].astype(BF16), tables[j][:, HD:], preferred_element_type=F32)
        got = (got / total).astype(BF16)
        attb[x, xa] = jnp.concatenate([got[:BLK], got[BLK:]], axis=1)

    def at_copy(d):
        return remote(attb.at[x], attb.at[x], at_s.at[d - 1], at_r.at[3 - d], at_x(d))

    def at_arrival(d):
        ref = attb.at[(x + d) % NX]
        return remote(ref, ref, at_s.at[d - 1], at_r.at[d - 1], at_x(d))

    for d in (1, 3, 2):
        at_copy(d).start()
    for cp in own_wo:
        cp.wait()
    for e in range(4):
        oc_arrival(e).wait_recv()

    order = (0, 1, 3, 2)

    def term(d, shard):
        b = (x + d) % NX
        a = jnp.dot(attb[b, x], wob[0, shard], preferred_element_type=F32)
        for e in range(1, NX):
            a = a + jnp.dot(attb[b, (x + e) % NX], wob[e, shard], preferred_element_type=F32)
        return a

    def r_copy(way, k, d):
        step = 1 if way == 0 else -1
        return remote(
            rsend.at[way, k - 1, d], rrecv.at[way, k - 1, d], rs_s.at[way, k - 1, d], rs_r.at[way, k - 1, d], at_z(step)
        )

    def long_way(i):
        return i % 2

    def r_step(way, k, d, longest):
        step = 1 if way == 0 else -1
        v = term(d, (z + step * k + NZ) % NZ)
        if k < longest:
            r_copy(way, k + 1, d).wait_recv()
            v = v + rrecv[way, k, d].astype(F32)
        rsend[way, k - 1, d] = v.astype(BF16)
        r_copy(way, k, d).start()

    sent = []
    for t in range(8):
        for i, d in enumerate(order):
            stage = t - i
            if stage < 0 or stage > 4:
                continue
            far = long_way(i)
            if stage == 0 and d > 0:
                at_arrival(d).wait_recv()
            if stage < 4:
                r_step(far, 4 - stage, d, 4)
                sent.append((far, 4 - stage, d))
            if stage < 3:
                r_step(1 - far, 3 - stage, d, 3)
                sent.append((1 - far, 3 - stage, d))
            if stage == 4:
                v = term(d, z)
                for way in range(2):
                    r_copy(way, 1, d).wait_recv()
                    v = v + rrecv[way, 0, d].astype(F32)
                out[pl.ds(pl.multiple_of(((x + d) % NX) * BLK, BLK), BLK), :] = v.astype(BF16)

    for way, k, d in sent:
        r_copy(way, k, d).wait_send()
    for b in range(4):
        for way in range(2):
            for hop in range(4):
                if x_used(way, hop, b):
                    x_copy(way, hop, b).wait_send()
    for i in range(2):
        for d in (1, 2, 3):
            w_copy(i, d).wait_send()
            o_copy(i, d).wait_send()
        for x2 in range(NX):
            cp = p_copy(i, x2)[0]

            @pl.when(jnp.logical_not(p_self(x2)))
            def _():
                cp.wait_send()

    for d in (1, 2, 3):
        ssx_copy(d).wait_send()
        kv_copy(d).wait_send()
        ka_copy(d).wait_send()
        at_copy(d).wait_send()
        ky_copy(d).wait_send()
        for xa in range(NX):
            q_copy(xa, d).wait_send()
    for k in range(1, NZ):
        ssz_copy(k).wait_send()
    for e in (1, 3):
        wy_copy(e).wait_send()
        oy_copy(e).wait_send()
    for e in range(4):
        wc_copy(e).wait_send()
        oc_copy(e).wait_send()
        kc_copy(e).wait_send()


def local(tokens, norm_gain, query_weight, pair_weight, ancestors, out_weight):
    dma = pltpu.SemaphoreType.DMA
    any_ = pl.BlockSpec(memory_space=pl.ANY)
    vmem = pl.BlockSpec(memory_space=pltpu.VMEM)
    vm = pltpu.VMEM
    return pl.pallas_call(
        kernel,
        out_shape=jax.ShapeDtypeStruct((512, 256), BF16),
        in_specs=[pl.BlockSpec(memory_space=pltpu.SMEM), vmem, any_, any_, any_, any_],
        out_specs=vmem,
        scratch_shapes=[
            vm((8, 512, 256), BF16),
            vm((512, 2048), BF16),
            vm((4, 128, 128), F32),
            vm((4, 8, 128), F32),
            vm((8, 8, 128), F32),
            vm((5, 8, 256, 256), BF16),
            vm((4, 8, 256, 256), BF16),
            vm((4, 128, 256), BF16),
            vm((3, 128, 256), BF16),
            vm((4, 128, 256), F32),
            vm((32, 128, 256), BF16),
            vm((4, 4, 128, 256), BF16),
            vm((3, 4, 128, 256), BF16),
            vm((4, 4, 128, 256), F32),
            vm((4, 128, 256), BF16),
            vm((4, 4, 128, 256), BF16),
            vm((2, 4, 4, 128, 256), BF16),
            vm((2, 4, 4, 128, 256), BF16),
            dma((10,)),
            dma((2, 4, 4)), dma((2, 4, 4)), dma((3,)), dma((3,)), dma((7,)), dma((7,)),
            dma((2, 3)), dma((2, 3)), dma((2, 4)), dma((2, 4)), dma((2,)), dma((2,)), dma((4,)), dma((4,)),
            dma((2, 3)), dma((2, 3)), dma((2,)), dma((2,)), dma((4,)), dma((4,)),
            dma((3,)), dma((3,)), dma((3,)), dma((3,)), dma((3,)), dma((3,)), dma((4,)), dma((4,)),
            dma((4, 3)), dma((4, 3)), dma((3,)), dma((3,)), dma((2, 4, 4)), dma((2, 4, 4)),
        ],
        compiler_params=pltpu.CompilerParams(collective_id=0, has_side_effects=True, vmem_limit_bytes=50 << 20),
        cost_estimate=pl.CostEstimate(flops=6 * 10**9, bytes_accessed=10 << 20, transcendentals=10**6),
        name="tree_attention",
    )(
        ancestors,
        norm_gain.reshape(32, 256),
        tokens,
        query_weight.reshape(8, 4, 256, 256),
        pair_weight.T,
        out_weight,
    )


def solution(mesh):
    return jax.shard_map(
        local,
        mesh=mesh,
        in_specs=(P("seq", "mp"), P(), P(None, "mp"), P(None, "mp"), P(), P("mp", None)),
        out_specs=P("seq", "mp"),
        check_vma=False,
    )
```

time: 510 us -> 128 us (0.25)
  the two profiles are of different devices: /device:TPU:8 before, /device:TPU:38 now
where the time goes in v1:
time: 128 us
  Pallas kernels  123 us (96%)
  local copies, waits for them, and re-layouts  4.41 us (3%)
    pallas_call x1, Pallas kernels, local(): pl.pallas_call(kernel, out_shape=jax.ShapeDtypeStruct((512, 256), BF16),...  123 us
    unnamed x6, local copies, waits for them, and re-layouts  3.64 us

profile of v1, /device:TPU:38, one launch (start us, length us, event | category | flops | bytes accessed | tf_op | source)
XLA Modules:
  0.0 127.6 jit_solution(16962824015983771707)
XLA Ops:
  0.0 0.8 copy.7.anc
  0.8 0.8 reshape.6.gain
  1.5 0.0 copy-start
  1.6 1.2 copy-done
  2.8 0.0 copy-start.1
  2.8 0.9 copy-done.1
  3.7 123.2 %tree_attention.1 = bf16[512,256]{1,0:T(8,128)(2,1)S(1)} custom-call(s32[32,5]{1,0:T(8,128)S(1)} %copy.7.anc, f32[32,256]{1,0:T(8,128)S(1)} %reshape.6.gain, bf16[512,256]{1,0:T(8,128)(2,1)S(1)} %copy-done.1, bf16[8,4,256,256]{3,2,1,0:T(8,128)(2,1)} %bitcast.3, bf16[64,8192]{1,0:T(8,128)(2,1)S(1)} %bitcast.2, bf16[256,8192]{1,0:T(8,128)(2,1)} %wo.1), custom_call_target="tpu_custom_call" | custom-call | flops 6000000000 | bytes 10485760 | tf_op jit(solution)/shard_map/tree_attention/pallas_call | solution.py:488
  126.9 0.7 copy.9
Async XLA Ops:
  1.5 1.2 copy-start
  2.8 0.9 copy-start.1

commit v2 on v1

--- a/solution.py
+++ b/solution.py
@@ -26,9 +26,9 @@
     anc, gain, tok, wq, pwt, wo, out,
     xg, xn, rcol, ssx, ssz, wb, wob, kvs, kvr, kvown, kvtab, qs, qr, qown, qb, attb, rsend, rrecv,
     local_sem, x_s, x_r, ssx_s, ssx_r, ssz_s, ssz_r,
-    w_s, w_r, p_s, p_r, wy_s, wy_r, wc_s, wc_r,
+    w_s, w_r, p_s, p_r, wy_s, wy_r, wf_s, wf_r, wc_s, wc_r,
     o_s, o_r, oy_s, oy_r, oc_s, oc_r,
-    kv_s, kv_r, ka_s, ka_r, ky_s, ky_r, kc_s, kc_r, q_s, q_r, at_s, at_r, rs_s, rs_r,
+    kv_s, kv_r, ka_s, ka_r, ky_s, ky_r, kc_s, kc_r, q_s, q_r, at_s, at_r, af_s, af_r, rs_s, rs_r,
 ):
     s = lax.axis_index("seq")
     m = lax.axis_index("mp")
@@ -102,31 +102,26 @@
         strip = lane_strip(2 * i)
         return remote(wq.at[strip, (x + d) % NX], wb.at[4 - d, strip], w_s.at[i, d - 1], w_r.at[i, 3 - d], at_x(d))
 
-    def p_copy(i, x2):
-        strip = lane_strip(2 * i)
-        src = pwt.at[:, pl.ds(pl.multiple_of((strip * NX + x2) * 256, 256), 256)]
-        dst = wb.at[4, strip, pl.ds(pl.multiple_of(pair_q * 64, 64), 64), :]
-        return remote(src, dst, p_s.at[i, x2], p_r.at[i, pair_q], (s, pair_z * NX + x2)), src, dst
+    def p_copy(x2):
+        src = pwt.at[:, pl.ds(pl.multiple_of((s * NX + x2) * 256, 256), 256)]
+        dst = wb.at[4, s, pl.ds(pl.multiple_of(pair_q * 64, 64), 64), :]
+        return remote(src, dst, p_s.at[x2], p_r.at[pair_q], (s, pair_z * NX + x2)), src, dst
 
     def p_self(x2):
         return jnp.logical_and(pair_z == z, x == x2)
 
-    def p_start(i):
-        for x2 in range(NX):
-            cp, src, dst = p_copy(i, x2)
-
-            @pl.when(p_self(x2))
-            def _():
-                pltpu.make_async_copy(src, dst, p_r.at[i, pair_q]).start()
-
-            @pl.when(jnp.logical_not(p_self(x2)))
-            def _():
-                cp.start()
-
-    for i in range(2):
-        for d in (1, 3, 2):
-            w_copy(i, d).start()
-        p_start(i)
+    for d in (1, 3, 2):
+        w_copy(0, d).start()
+    for x2 in range(NX):
+        cp, src, dst = p_copy(x2)
+
+        @pl.when(p_self(x2))
+        def _():
+            pltpu.make_async_copy(src, dst, p_r.at[pair_q]).start()
+
+        @pl.when(jnp.logical_not(p_self(x2)))
+        def _():
+            cp.start()
 
     own_x.wait()
     row_id = lax.broadcasted_iota(jnp.int32, (8, BLK), 0)
@@ -146,51 +141,68 @@
     for d in (1, 3, 2):
         ssx_copy(d).start()
 
-    def x_forward(hop):
-        for b in range(4):
+    def x_forward(hop, blocks=range(4)):
+        for b in blocks:
             for way in range(2):
                 if x_used(way, hop, b):
                     x_arrival(way, hop, b).wait_recv()
                     if hop < 3 and x_used(way, hop + 1, b):
                         x_copy(way, hop + 1, b).start()
 
-    x_forward(0)
+    def wy_copy(e, d):
+        src = wb.at[d, s]
+        return remote(src, src, wy_s.at[e // 2, d - 1], wy_r.at[(3 - e) // 2, d - 1], at_y(e))
+
+    def wy_arrival(e, d):
+        ref = wb.at[d, lane_strip(e)]
+        return remote(ref, ref, wy_s.at[e // 2, d - 1], wy_r.at[e // 2, d - 1], at_y(e))
+
+    def wf_copy():
+        src = wb.at[4, s]
+        return remote(src, src, wf_s, wf_r, at_y(2))
+
+    def wf_arrival():
+        ref = wb.at[4, lane_strip(2)]
+        return remote(ref, ref, wf_s, wf_r, at_y(2))
+
+    def wc_copy(e, d):
+        src = wb.at[d, lane_strip(e)]
+        return remote(src, src, wc_s.at[e, d - 1], wc_r.at[e, d - 1], sibling)
+
+    def wc_arrival(e, d):
+        ref = wb.at[d, far_strip(e)]
+        return remote(ref, ref, wc_s.at[e, d - 1], wc_r.at[e, d - 1], sibling)
+
+    def w_arrive(i, d):
+        ref = wb.at[d, lane_strip(2 * i)]
+        remote(ref, ref, w_s.at[i, d - 1], w_r.at[i, d - 1], at_x(d)).wait_recv()
+
+    def w_pass(d):
+        for e in (1, 3):
+            wy_copy(e, d).start()
+        wc_copy(0, d).start()
+
+    x_forward(0, (0, 1))
     for d in (1, 2, 3):
         ssx_copy(d).wait_recv()
     ssz[0] = ssx[0] + ssx[1] + ssx[2] + ssx[3]
     for k in (1, 7, 2, 6, 3, 5, 4):
         ssz_copy(k).start()
-
-    def wy_copy(e):
-        src = wb.at[pl.ds(1, 4), s]
-        return remote(src, src, wy_s.at[e // 2], wy_r.at[(3 - e) // 2], at_y(e))
-
-    def wy_arrival(e):
-        ref = wb.at[pl.ds(1, 4), lane_strip(e)]
-        return remote(ref, ref, wy_s.at[e // 2], wy_r.at[e // 2], at_y(e))
-
-    def wc_copy(e):
-        src = wb.at[pl.ds(1, 4), lane_strip(e)]
-        return remote(src, src, wc_s.at[e], wc_r.at[e], sibling)
-
-    def wc_arrival(e):
-        ref = wb.at[pl.ds(1, 4), far_strip(e)]
-        return remote(ref, ref, wc_s.at[e], wc_r.at[e], sibling)
-
-    def w_arrive(i):
-        strip = lane_strip(2 * i)
-        for d in (1, 2, 3):
-            ref = wb.at[d, strip]
-            remote(ref, ref, w_s.at[i, d - 1], w_r.at[i, d - 1], at_x(d)).wait_recv()
-        for q in range(4):
-            ref = wb.at[4, strip, pl.ds(q * 64, 64), :]
-            remote(ref, ref, p_s.at[i, q], p_r.at[i, q], sibling).wait_recv()
-
-    w_arrive(0)
-    wy_copy(1).start()
-    wy_copy(3).start()
-    wc_copy(0).start()
-    x_forward(1)
+    for d in (1, 3):
+        w_arrive(0, d)
+        w_pass(d)
+    for d in (1, 3, 2):
+        w_copy(1, d).start()
+    x_forward(0, (2, 3))
+    w_arrive(0, 2)
+    w_pass(2)
+    x_forward(1, (0, 1))
+    for q in range(4):
+        ref = wb.at[4, s, pl.ds(q * 64, 64), :]
+        remote(ref, ref, p_s.at[q], p_r.at[q], sibling).wait_recv()
+    w_pass(4)
+    wf_copy().start()
+    x_forward(1, (2, 3))
 
     for k in range(1, NZ):
         ssz_copy(k).wait_recv()
@@ -202,7 +214,8 @@
         rcol[b] = jnp.broadcast_to(scale[b : b + 1, :], (BLK, BLK)).T
 
     def normalise(shard):
-        g = gain[pl.ds(shard * NX + x, 1), :]
+        row = (shard * NX + x) * 2
+        g = jnp.concatenate([gain[pl.ds(row, 1), :], gain[pl.ds(row + 1, 1), :]], axis=1)
 
         def one(b, carry):
             at = pl.ds(pl.multiple_of(b * BLK, BLK), BLK)
@@ -216,8 +229,9 @@
     normalise(z)
     normalise((z + 1) % NZ)
     normalise((z + 7) % NZ)
-    w_arrive(1)
-    wc_copy(2).start()
+    for d in (1, 3, 2):
+        w_arrive(1, d)
+        wc_copy(2, d).start()
 
     def wo_block(strip, x2):
         return wo.at[:, pl.ds(pl.multiple_of((strip * NX + x2) * 256, 256), 256)]
@@ -252,22 +266,31 @@
             ref = wob.at[d, strip]
             remote(ref, ref, o_s.at[i, d - 1], o_r.at[i, d - 1], at_x(d)).wait_recv()
 
-    for i in range(2):
-        for d in (1, 3, 2):
-            o_copy(i, d).start()
+    for d in (1, 3, 2):
+        o_copy(0, d).start()
 
     x_forward(2)
+    for d in (1, 3, 2):
+        o_copy(1, d).start()
     normalise((z + 2) % NZ)
     normalise((z + 6) % NZ)
-    for e in (1, 3):
-        wy_arrival(e).wait_recv()
-        wc_copy(e).start()
+    for d in (1, 3, 2, 4):
+        for e in (1, 3):
+            wy_arrival(e, d).wait_recv()
+            wc_copy(e, d).start()
+    wf_arrival().wait_recv()
+    wc_copy(2, 4).start()
     normalise((z + 3) % NZ)
     normalise((z + 5) % NZ)
+    o_arrive(0)
+    oy_copy(1).start()
+    oy_copy(3).start()
+    oc_copy(0).start()
     x_forward(3)
     normalise((z + 4) % NZ)
     for e in range(4):
-        wc_arrival(e).wait_recv()
+        for d in range(1, 5):
+            wc_arrival(e, d).wait_recv()
     own_w.wait()
 
     acc = nt_dot(xn[:, :256], wb[4, 0])
@@ -290,8 +313,6 @@
         a = jnp.dot(xn[...], wb[d].reshape(2048, 256), preferred_element_type=F32).reshape(4, BLK, 256)
         qs[xa] = a.astype(BF16)
         qown[xa] = a
-        for e in (1, 3, 2):
-            q_copy(xa, e).start()
         return carry
 
     lax.fori_loop(0, 4, q_part, 0)
@@ -309,22 +330,16 @@
         ref = kvtab.at[s * NX + (x + d) % NX]
         return remote(ref, ref, ka_s.at[d - 1], ka_r.at[d - 1], at_x(d))
 
-    for d in (1, 3, 2):
-        ka_copy(d).start()
-    o_arrive(0)
-    oy_copy(1).start()
-    oy_copy(3).start()
-    oc_copy(0).start()
+    def ky_copy(e, d):
+        ref = kvtab.at[s * NX + (x + d) % NX]
+        return remote(ref, ref, ky_s.at[e - 1, d], ky_r.at[3 - e, d], at_y(e))
+
+    def ky_arrival(e, d):
+        ref = kvtab.at[lane_strip(e) * NX + (x + d) % NX]
+        return remote(ref, ref, ky_s.at[e - 1, d], ky_r.at[e - 1, d], at_y(e))
 
     def group(strip):
         return kvtab.at[pl.ds(strip * NX, NX)]
-
-    def ky_copy(e):
-        return remote(group(s), group(s), ky_s.at[e - 1], ky_r.at[3 - e], at_y(e))
-
-    def ky_arrival(e):
-        ref = group(lane_strip(e))
-        return remote(ref, ref, ky_s.at[e - 1], ky_r.at[e - 1], at_y(e))
 
     def kc_copy(e):
         ref = group(lane_strip(e))
@@ -335,13 +350,30 @@
         return remote(ref, ref, kc_s.at[e], kc_r.at[e], sibling)
 
     for d in (1, 3, 2):
+        ka_copy(d).start()
+    for e in (1, 3, 2):
+        ky_copy(e, 0).start()
+    for d in (1, 3):
         ka_arrival(d).wait_recv()
+        for e in (1, 3, 2):
+            ky_copy(e, d).start()
+    for xa in range(NX):
+        for e in (1, 3, 2):
+            q_copy(xa, e).start()
+    ka_arrival(2).wait_recv()
     for e in (1, 3, 2):
-        ky_copy(e).start()
+        ky_copy(e, 2).start()
     kc_copy(0).start()
 
     o_arrive(1)
     oc_copy(2).start()
+    for e in (1, 3):
+        oy_arrival(e).wait_recv()
+        oc_copy(e).start()
+    for e in (1, 3, 2):
+        for d in (0, 1, 3, 2):
+            ky_arrival(e, d).wait_recv()
+        kc_copy(e).start()
 
     for xa in range(NX):
         for d in (1, 2, 3):
@@ -349,16 +381,10 @@
         v = qown[xa, x] + qr[0, xa].astype(F32) + qr[1, xa].astype(F32) + qr[2, xa].astype(F32)
         qb[xa] = v.astype(BF16)
 
-    for e in (1, 3):
-        oy_arrival(e).wait_recv()
-        oc_copy(e).start()
-    for e in (1, 3, 2):
-        ky_arrival(e).wait_recv()
-        kc_copy(e).start()
     for e in range(4):
         kc_arrival(e).wait_recv()
 
-    listed = [anc[block, j] for j in range(5)]
+    listed = [anc[j, block] for j in range(5)]
     tables = [kvtab[jnp.maximum(i, 0)] for i in listed] + [kvtab[block]]
     causal = lax.broadcasted_iota(jnp.int32, (BLK, BLK), 0) >= lax.broadcasted_iota(jnp.int32, (BLK, BLK), 1)
     causal = jnp.concatenate([causal, causal], axis=0)
@@ -380,19 +406,45 @@
         got = (got / total).astype(BF16)
         attb[x, xa] = jnp.concatenate([got[:BLK], got[BLK:]], axis=1)
 
-    def at_copy(d):
-        return remote(attb.at[x], attb.at[x], at_s.at[d - 1], at_r.at[3 - d], at_x(d))
-
-    def at_arrival(d):
-        ref = attb.at[(x + d) % NX]
-        return remote(ref, ref, at_s.at[d - 1], at_r.at[d - 1], at_x(d))
-
-    for d in (1, 3, 2):
-        at_copy(d).start()
+    def half(b, h):
+        return attb.at[b, pl.ds(2 * h, 2)]
+
+    def at_copy(d, h):
+        return remote(half(x, h), half(x, h), at_s.at[d // 2, h], at_r.at[(3 - d) // 2, h], at_x(d))
+
+    def at_arrival(d, h):
+        ref = half((x + d) % NX, h)
+        return remote(ref, ref, at_s.at[d // 2, h], at_r.at[d // 2, h], at_x(d))
+
+    def af_copy(d):
+        h = 0 if d == 1 else 1
+        ref = half((x + 4 - d) % NX, h)
+        return remote(ref, ref, af_s.at[h], af_r.at[h], at_x(d))
+
+    def af_arrival(h):
+        ref = half((x + 2) % NX, h)
+        return remote(ref, ref, af_s.at[h], af_r.at[h], at_x(1))
+
+    for h in range(2):
+        at_copy(1, h).start()
+        at_copy(3, 1 - h).start()
     for cp in own_wo:
         cp.wait()
     for e in range(4):
         oc_arrival(e).wait_recv()
+
+    def at_ready(d):
+        if d == 1:
+            at_arrival(3, 0).wait_recv()
+            af_copy(1).start()
+            at_arrival(1, 1).wait_recv()
+            af_copy(3).start()
+            at_arrival(1, 0).wait_recv()
+        elif d == 3:
+            at_arrival(3, 1).wait_recv()
+        elif d == 2:
+            af_arrival(0).wait_recv()
+            af_arrival(1).wait_recv()
 
     order = (0, 1, 3, 2)
 
@@ -403,10 +455,12 @@
             a = a + jnp.dot(attb[b, (x + e) % NX], wob[e, shard], preferred_element_type=F32)
         return a
 
-    def r_copy(way, k, d):
+    def r_copy(way, k, d, h):
         step = 1 if way == 0 else -1
+        at = pl.ds(h * 64, 64)
+        sem = (way, k - 1, d, h)
         return remote(
-            rsend.at[way, k - 1, d], rrecv.at[way, k - 1, d], rs_s.at[way, k - 1, d], rs_r.at[way, k - 1, d], at_z(step)
+            rsend.at[way, k - 1, d, at], rrecv.at[way, k - 1, d, at], rs_s.at[sem], rs_r.at[sem], at_z(step)
         )
 
     def long_way(i):
@@ -415,11 +469,14 @@
     def r_step(way, k, d, longest):
         step = 1 if way == 0 else -1
         v = term(d, (z + step * k + NZ) % NZ)
-        if k < longest:
-            r_copy(way, k + 1, d).wait_recv()
-            v = v + rrecv[way, k, d].astype(F32)
-        rsend[way, k - 1, d] = v.astype(BF16)
-        r_copy(way, k, d).start()
+        for h in range(2):
+            at = slice(h * 64, h * 64 + 64)
+            u = v[at]
+            if k < longest:
+                r_copy(way, k + 1, d, h).wait_recv()
+                u = u + rrecv[way, k, d, at].astype(F32)
+            rsend[way, k - 1, d, at] = u.astype(BF16)
+            r_copy(way, k, d, h).start()
 
     sent = []
     for t in range(8):
@@ -428,8 +485,8 @@
             if stage < 0 or stage > 4:
                 continue
             far = long_way(i)
-            if stage == 0 and d > 0:
-                at_arrival(d).wait_recv()
+            if stage == 0:
+                at_ready(d)
             if stage < 4:
                 r_step(far, 4 - stage, d, 4)
                 sent.append((far, 4 - stage, d))
@@ -438,13 +495,17 @@
                 sent.append((1 - far, 3 - stage, d))
             if stage == 4:
                 v = term(d, z)
-                for way in range(2):
-                    r_copy(way, 1, d).wait_recv()
-                    v = v + rrecv[way, 0, d].astype(F32)
-                out[pl.ds(pl.multiple_of(((x + d) % NX) * BLK, BLK), BLK), :] = v.astype(BF16)
+                for h in range(2):
+                    at = slice(h * 64, h * 64 + 64)
+                    u = v[at]
+                    for way in range(2):
+                        r_copy(way, 1, d, h).wait_recv()
+                        u = u + rrecv[way, 0, d, at].astype(F32)
+                    out[pl.ds(pl.multiple_of(((x + d) % NX) * BLK + h * 64, 64), 64), :] = u.astype(BF16)
 
     for way, k, d in sent:
-        r_copy(way, k, d).wait_send()
+        r_copy(way, k, d, 0).wait_send()
+        r_copy(way, k, d, 1).wait_send()
     for b in range(4):
         for way in range(2):
             for hop in range(4):
@@ -454,28 +515,35 @@
         for d in (1, 2, 3):
             w_copy(i, d).wait_send()
             o_copy(i, d).wait_send()
-        for x2 in range(NX):
-            cp = p_copy(i, x2)[0]
-
-            @pl.when(jnp.logical_not(p_self(x2)))
-            def _():
-                cp.wait_send()
+    for x2 in range(NX):
+        cp = p_copy(x2)[0]
+
+        @pl.when(jnp.logical_not(p_self(x2)))
+        def _():
+            cp.wait_send()
 
     for d in (1, 2, 3):
         ssx_copy(d).wait_send()
         kv_copy(d).wait_send()
         ka_copy(d).wait_send()
-        at_copy(d).wait_send()
-        ky_copy(d).wait_send()
         for xa in range(NX):
             q_copy(xa, d).wait_send()
+        for e in range(4):
+            ky_copy(d, e).wait_send()
+    for d in (1, 3):
+        af_copy(d).wait_send()
+        for h in range(2):
+            at_copy(d, h).wait_send()
     for k in range(1, NZ):
         ssz_copy(k).wait_send()
+    wf_copy().wait_send()
     for e in (1, 3):
-        wy_copy(e).wait_send()
+        for d in range(1, 5):
+            wy_copy(e, d).wait_send()
         oy_copy(e).wait_send()
     for e in range(4):
-        wc_copy(e).wait_send()
+        for d in range(1, 5):
+            wc_copy(e, d).wait_send()
         oc_copy(e).wait_send()
         kc_copy(e).wait_send()
 
@@ -511,17 +579,17 @@
             vm((2, 4, 4, 128, 256), BF16),
             dma((10,)),
             dma((2, 4, 4)), dma((2, 4, 4)), dma((3,)), dma((3,)), dma((7,)), dma((7,)),
-            dma((2, 3)), dma((2, 3)), dma((2, 4)), dma((2, 4)), dma((2,)), dma((2,)), dma((4,)), dma((4,)),
+            dma((2, 3)), dma((2, 3)), dma((4,)), dma((4,)), dma((2, 4)), dma((2, 4)), dma(()), dma(()), dma((4, 4)), dma((4, 4)),
             dma((2, 3)), dma((2, 3)), dma((2,)), dma((2,)), dma((4,)), dma((4,)),
-            dma((3,)), dma((3,)), dma((3,)), dma((3,)), dma((3,)), dma((3,)), dma((4,)), dma((4,)),
-            dma((4, 3)), dma((4, 3)), dma((3,)), dma((3,)), dma((2, 4, 4)), dma((2, 4, 4)),
+            dma((3,)), dma((3,)), dma((3,)), dma((3,)), dma((3, 4)), dma((3, 4)), dma((4,)), dma((4,)),
+            dma((4, 3)), dma((4, 3)), dma((2, 2)), dma((2, 2)), dma((2,)), dma((2,)), dma((2, 4, 4, 2)), dma((2, 4, 4, 2)),
         ],
-        compiler_params=pltpu.CompilerParams(collective_id=0, has_side_effects=True, vmem_limit_bytes=50 << 20),
+        compiler_params=pltpu.CompilerParams(collective_id=0, has_side_effects=True, vmem_limit_bytes=60 << 20),
         cost_estimate=pl.CostEstimate(flops=6 * 10**9, bytes_accessed=10 << 20, transcendentals=10**6),
         name="tree_attention",
     )(
-        ancestors,
-        norm_gain.reshape(32, 256),
+        ancestors.T,
+        norm_gain.reshape(64, 128),
         tokens,
         query_weight.reshape(8, 4, 256, 256),
         pair_weight.T,

time: 128 us -> 103 us (0.80)
  the two profiles are of different devices: /device:TPU:38 before, /device:TPU:8 now
where the time goes in v2:
time: 103 us; the launch traced here: 102 us
  Pallas kernels  100 us (97%)
  local copies, waits for them, and re-layouts  1.67 us (2%)
    pallas_call x1, Pallas kernels, local(): pl.pallas_call(kernel, out_shape=jax.ShapeDtypeStruct((512, 256), BF16),...  100 us

profile of v2, /device:TPU:8, one launch (start us, length us, event | category | flops | bytes accessed | tf_op | source)
XLA Modules:
  0.0 101.7 jit_solution(14404953812185435870)
XLA Ops:
  0.0 100.1 %tree_attention.1 = bf16[512,256]{1,0:T(8,128)(2,1)} custom-call(s32[5,32]{1,0:T(8,128)} %bitcast.7, f32[64,128]{1,0:T(8,128)} %bitcast.6, bf16[512,256]{1,0:T(8,128)(2,1)} %tok.1, bf16[8,4,256,256]{3,2,1,0:T(8,128)(2,1)} %bitcast.4, bf16[64,8192]{1,0:T(8,128)(2,1)} %bitcast.5, bf16[256,8192]{1,0:T(8,128)(2,1)} %wo.1), custom_call_target="tpu_custom_call" | custom-call | flops 6000000000 | bytes 10485760 | tf_op jit(solution)/shard_map/tree_attention/pallas_call | solution.py:556
  100.1 1.7 %copy.8 = bf16[512,256]{1,0:T(8,128)(2,1)} copy(bf16[512,256]{1,0:T(8,128)(2,1)} %tree_attention.1) | data formatting | bytes 524288

commit v3 on v2

--- a/solution.py
+++ b/solution.py
@@ -28,7 +28,7 @@
     local_sem, x_s, x_r, ssx_s, ssx_r, ssz_s, ssz_r,
     w_s, w_r, p_s, p_r, wy_s, wy_r, wf_s, wf_r, wc_s, wc_r,
     o_s, o_r, oy_s, oy_r, oc_s, oc_r,
-    kv_s, kv_r, ka_s, ka_r, ky_s, ky_r, kc_s, kc_r, q_s, q_r, at_s, at_r, af_s, af_r, rs_s, rs_r,
+    kv_s, kv_r, ka_s, ka_r, ky_s, ky_r, kf_s, kf_r, kc_s, kc_r, q_s, q_r, at_s, at_r, af_s, af_r, rs_s, rs_r,
 ):
     s = lax.axis_index("seq")
     m = lax.axis_index("mp")
@@ -196,13 +196,53 @@
     x_forward(0, (2, 3))
     w_arrive(0, 2)
     w_pass(2)
-    x_forward(1, (0, 1))
+    def wo_block(strip, x2):
+        return wo.at[:, pl.ds(pl.multiple_of((strip * NX + x2) * 256, 256), 256)]
+
+    own_wo = [pltpu.make_async_copy(wo_block(k, x), wob.at[0, k], local_sem.at[2 + k]) for k in range(NZ)]
+    for cp in own_wo:
+        cp.start()
+
+    def o_copy(i, d):
+        strip = lane_strip(2 * i)
+        return remote(wo_block(strip, (x + d) % NX), wob.at[4 - d, strip], o_s.at[i, d - 1], o_r.at[i, 3 - d], at_x(d))
+
+    def oy_copy(e):
+        src = wob.at[pl.ds(1, 3), s]
+        return remote(src, src, oy_s.at[e // 2], oy_r.at[(3 - e) // 2], at_y(e))
+
+    def oy_arrival(e):
+        ref = wob.at[pl.ds(1, 3), lane_strip(e)]
+        return remote(ref, ref, oy_s.at[e // 2], oy_r.at[e // 2], at_y(e))
+
+    def oc_copy(e):
+        src = wob.at[pl.ds(1, 3), lane_strip(e)]
+        return remote(src, src, oc_s.at[e], oc_r.at[e], sibling)
+
+    def oc_arrival(e):
+        ref = wob.at[pl.ds(1, 3), far_strip(e)]
+        return remote(ref, ref, oc_s.at[e], oc_r.at[e], sibling)
+
+    def o_arrive(i):
+        strip = lane_strip(2 * i)
+        for d in (1, 2, 3):
+            ref = wob.at[d, strip]
+            remote(ref, ref, o_s.at[i, d - 1], o_r.at[i, d - 1], at_x(d)).wait_recv()
+
+    x_forward(1)
     for q in range(4):
         ref = wb.at[4, s, pl.ds(q * 64, 64), :]
         remote(ref, ref, p_s.at[q], p_r.at[q], sibling).wait_recv()
     w_pass(4)
     wf_copy().start()
-    x_forward(1, (2, 3))
+    for d in (1, 3, 2):
+        w_arrive(1, d)
+        wc_copy(2, d).start()
+    for d in (1, 3, 2):
+        o_copy(0, d).start()
+    x_forward(2)
+    for d in (1, 3, 2):
+        o_copy(1, d).start()
 
     for k in range(1, NZ):
         ssz_copy(k).wait_recv()
@@ -229,49 +269,6 @@
     normalise(z)
     normalise((z + 1) % NZ)
     normalise((z + 7) % NZ)
-    for d in (1, 3, 2):
-        w_arrive(1, d)
-        wc_copy(2, d).start()
-
-    def wo_block(strip, x2):
-        return wo.at[:, pl.ds(pl.multiple_of((strip * NX + x2) * 256, 256), 256)]
-
-    own_wo = [pltpu.make_async_copy(wo_block(k, x), wob.at[0, k], local_sem.at[2 + k]) for k in range(NZ)]
-    for cp in own_wo:
-        cp.start()
-
-    def o_copy(i, d):
-        strip = lane_strip(2 * i)
-        return remote(wo_block(strip, (x + d) % NX), wob.at[4 - d, strip], o_s.at[i, d - 1], o_r.at[i, 3 - d], at_x(d))
-
-    def oy_copy(e):
-        src = wob.at[pl.ds(1, 3), s]
-        return remote(src, src, oy_s.at[e // 2], oy_r.at[(3 - e) // 2], at_y(e))
-
-    def oy_arrival(e):
-        ref = wob.at[pl.ds(1, 3), lane_strip(e)]
-        return remote(ref, ref, oy_s.at[e // 2], oy_r.at[e // 2], at_y(e))
-
-    def oc_copy(e):
-        src = wob.at[pl.ds(1, 3), lane_strip(e)]
-        return remote(src, src, oc_s.at[e], oc_r.at[e], sibling)
-
-    def oc_arrival(e):
-        ref = wob.at[pl.ds(1, 3), far_strip(e)]
-        return remote(ref, ref, oc_s.at[e], oc_r.at[e], sibling)
-
-    def o_arrive(i):
-        strip = lane_strip(2 * i)
-        for d in (1, 2, 3):
-            ref = wob.at[d, strip]
-            remote(ref, ref, o_s.at[i, d - 1], o_r.at[i, d - 1], at_x(d)).wait_recv()
-
-    for d in (1, 3, 2):
-        o_copy(0, d).start()
-
-    x_forward(2)
-    for d in (1, 3, 2):
-        o_copy(1, d).start()
     normalise((z + 2) % NZ)
     normalise((z + 6) % NZ)
     for d in (1, 3, 2, 4):
@@ -282,16 +279,10 @@
     wc_copy(2, 4).start()
     normalise((z + 3) % NZ)
     normalise((z + 5) % NZ)
-    o_arrive(0)
-    oy_copy(1).start()
-    oy_copy(3).start()
-    oc_copy(0).start()
     x_forward(3)
     normalise((z + 4) % NZ)
     for e in range(4):
-        for d in range(1, 5):
-            wc_arrival(e, d).wait_recv()
-    own_w.wait()
+        wc_arrival(e, 4).wait_recv()
 
     acc = nt_dot(xn[:, :256], wb[4, 0])
     for k in range(1, NZ):
@@ -305,6 +296,64 @@
     for d in (1, 3, 2):
         kv_copy(d).start()
 
+    o_arrive(0)
+    oy_copy(1).start()
+    oy_copy(3).start()
+    oc_copy(0).start()
+
+    block = s * NX + x
+    for d in (1, 3, 2):
+        kv_copy(d).wait_recv()
+    mine = kvown[x] + kvr[0].astype(F32) + kvr[1].astype(F32) + kvr[2].astype(F32)
+    kvtab[block] = mine.astype(BF16)
+
+    def ka_copy(d):
+        return remote(kvtab.at[block], kvtab.at[block], ka_s.at[d - 1], ka_r.at[3 - d], at_x(d))
+
+    def ka_arrival(d):
+        ref = kvtab.at[s * NX + (x + d) % NX]
+        return remote(ref, ref, ka_s.at[d - 1], ka_r.at[d - 1], at_x(d))
+
+    def ky_copy(e, d):
+        ref = kvtab.at[s * NX + (x + d) % NX]
+        return remote(ref, ref, ky_s.at[e // 2, d], ky_r.at[(3 - e) // 2, d], at_y(e))
+
+    def ky_arrival(e, d):
+        ref = kvtab.at[lane_strip(e) * NX + (x + d) % NX]
+        return remote(ref, ref, ky_s.at[e // 2, d], ky_r.at[e // 2, d], at_y(e))
+
+    def kf_half(strip, d, i):
+        return kvtab.at[strip * NX + (x + d) % NX, pl.ds((1 - i) * 64, 64)]
+
+    def kf_copy(e, d):
+        ref = kf_half(lane_strip(e), d, e // 2)
+        return remote(ref, ref, kf_s.at[e // 2, d], kf_r.at[e // 2, d], at_y(4 - e))
+
+    def kf_arrival(i, d):
+        ref = kf_half(lane_strip(2), d, i)
+        return remote(ref, ref, kf_s.at[i, d], kf_r.at[i, d], at_y(1))
+
+    def group(strip):
+        return kvtab.at[pl.ds(strip * NX, NX)]
+
+    def kc_copy(e):
+        ref = group(lane_strip(e))
+        return remote(ref, ref, kc_s.at[e], kc_r.at[e], sibling)
+
+    def kc_arrival(e):
+        ref = group(far_strip(e))
+        return remote(ref, ref, kc_s.at[e], kc_r.at[e], sibling)
+
+    def ky_pass(d):
+        for e in (1, 3):
+            ky_arrival(e, d).wait_recv()
+            kf_copy(e, d).start()
+
+    for d in (1, 3, 2):
+        ka_copy(d).start()
+    for e in (1, 3):
+        ky_copy(e, 0).start()
+
     def q_copy(xa, d):
         return remote(qs.at[xa, (x + d) % NX], qr.at[3 - d, xa], q_s.at[xa, d - 1], q_r.at[xa, 3 - d], at_x(d))
 
@@ -313,67 +362,39 @@
         a = jnp.dot(xn[...], wb[d].reshape(2048, 256), preferred_element_type=F32).reshape(4, BLK, 256)
         qs[xa] = a.astype(BF16)
         qown[xa] = a
+        for e in (1, 3, 2):
+            q_copy(xa, e).start()
         return carry
 
+    own_w.wait()
+    for e in range(4):
+        for d in range(1, 4):
+            wc_arrival(e, d).wait_recv()
     lax.fori_loop(0, 4, q_part, 0)
 
-    block = s * NX + x
-    for d in (1, 2, 3):
-        kv_copy(d).wait_recv()
-    mine = kvown[x] + kvr[0].astype(F32) + kvr[1].astype(F32) + kvr[2].astype(F32)
-    kvtab[block] = mine.astype(BF16)
-
-    def ka_copy(d):
-        return remote(kvtab.at[block], kvtab.at[block], ka_s.at[d - 1], ka_r.at[3 - d], at_x(d))
-
-    def ka_arrival(d):
-        ref = kvtab.at[s * NX + (x + d) % NX]
-        return remote(ref, ref, ka_s.at[d - 1], ka_r.at[d - 1], at_x(d))
-
-    def ky_copy(e, d):
-        ref = kvtab.at[s * NX + (x + d) % NX]
-        return remote(ref, ref, ky_s.at[e - 1, d], ky_r.at[3 - e, d], at_y(e))
-
-    def ky_arrival(e, d):
-        ref = kvtab.at[lane_strip(e) * NX + (x + d) % NX]
-        return remote(ref, ref, ky_s.at[e - 1, d], ky_r.at[e - 1, d], at_y(e))
-
-    def group(strip):
-        return kvtab.at[pl.ds(strip * NX, NX)]
-
-    def kc_copy(e):
-        ref = group(lane_strip(e))
-        return remote(ref, ref, kc_s.at[e], kc_r.at[e], sibling)
-
-    def kc_arrival(e):
-        ref = group(far_strip(e))
-        return remote(ref, ref, kc_s.at[e], kc_r.at[e], sibling)
-
-    for d in (1, 3, 2):
-        ka_copy(d).start()
-    for e in (1, 3, 2):
-        ky_copy(e, 0).start()
     for d in (1, 3):
         ka_arrival(d).wait_recv()
-        for e in (1, 3, 2):
+        for e in (1, 3):
             ky_copy(e, d).start()
-    for xa in range(NX):
-        for e in (1, 3, 2):
-            q_copy(xa, e).start()
+    ky_pass(0)
     ka_arrival(2).wait_recv()
-    for e in (1, 3, 2):
+    for e in (1, 3):
         ky_copy(e, 2).start()
     kc_copy(0).start()
-
+    for d in (1, 3):
+        ky_pass(d)
     o_arrive(1)
     oc_copy(2).start()
     for e in (1, 3):
         oy_arrival(e).wait_recv()
         oc_copy(e).start()
-    for e in (1, 3, 2):
-        for d in (0, 1, 3, 2):
-            ky_arrival(e, d).wait_recv()
-        kc_copy(e).start()
+    ky_pass(2)
+    kc_copy(1).start()
+    kc_copy(3).start()
+    for d in (0, 1, 3, 2):
+        for i in range(2):
+            kf_arrival(i, d).wait_recv()
+    kc_copy(2).start()
 
     for xa in range(NX):
         for d in (1, 2, 3):
@@ -446,8 +467,6 @@
             af_arrival(0).wait_recv()
             af_arrival(1).wait_recv()
 
-    order = (0, 1, 3, 2)
-
     def term(d, shard):
         b = (x + d) % NX
         a = jnp.dot(attb[b, x], wob[0, shard], preferred_element_type=F32)
@@ -463,8 +482,7 @@
             rsend.at[way, k - 1, d, at], rrecv.at[way, k - 1, d, at], rs_s.at[sem], rs_r.at[sem], at_z(step)
         )
 
-    def long_way(i):
-        return i % 2
+    long_way = {0: 0, 1: 1, 3: 0, 2: 1}
 
     def r_step(way, k, d, longest):
         step = 1 if way == 0 else -1
@@ -479,29 +497,29 @@
             r_copy(way, k, d, h).start()
 
     sent = []
-    for t in range(8):
-        for i, d in enumerate(order):
-            stage = t - i
-            if stage < 0 or stage > 4:
-                continue
-            far = long_way(i)
-            if stage == 0:
-                at_ready(d)
-            if stage < 4:
-                r_step(far, 4 - stage, d, 4)
-                sent.append((far, 4 - stage, d))
-            if stage < 3:
-                r_step(1 - far, 3 - stage, d, 3)
-                sent.append((1 - far, 3 - stage, d))
-            if stage == 4:
-                v = term(d, z)
-                for h in range(2):
-                    at = slice(h * 64, h * 64 + 64)
-                    u = v[at]
-                    for way in range(2):
-                        r_copy(way, 1, d, h).wait_recv()
-                        u = u + rrecv[way, 0, d, at].astype(F32)
-                    out[pl.ds(pl.multiple_of(((x + d) % NX) * BLK + h * 64, 64), 64), :] = u.astype(BF16)
+    schedule = (
+        (0, 0), (1, 0), (0, 1), (0, 3), (2, 0), (0, 2), (1, 1), (1, 3), (3, 0), (1, 2),
+        (2, 1), (2, 3), (4, 0), (2, 2), (3, 1), (3, 3), (3, 2), (4, 1), (4, 3), (4, 2),
+    )
+    for stage, d in schedule:
+        far = long_way[d]
+        if stage == 0:
+            at_ready(d)
+        if stage < 4:
+            r_step(far, 4 - stage, d, 4)
+            sent.append((far, 4 - stage, d))
+        if stage < 3:
+            r_step(1 - far, 3 - stage, d, 3)
+            sent.append((1 - far, 3 - stage, d))
+        if stage == 4:
+            v = term(d, z)
+            for h in range(2):
+                at = slice(h * 64, h * 64 + 64)
+                u = v[at]
+                for way in range(2):
+                    r_copy(way, 1, d, h).wait_recv()
+                    u = u + rrecv[way, 0, d, at].astype(F32)
+                out[pl.ds(pl.multiple_of(((x + d) % NX) * BLK + h * 64, 64), 64), :] = u.astype(BF16)
 
     for way, k, d in sent:
         r_copy(way, k, d, 0).wait_send()
@@ -528,8 +546,6 @@
         ka_copy(d).wait_send()
         for xa in range(NX):
             q_copy(xa, d).wait_send()
-        for e in range(4):
-            ky_copy(d, e).wait_send()
     for d in (1, 3):
         af_copy(d).wait_send()
         for h in range(2):
@@ -537,6 +553,10 @@
     for k in range(1, NZ):
         ssz_copy(k).wait_send()
     wf_copy().wait_send()
+    for e in (1, 3):
+        for d in range(4):
+            ky_copy(e, d).wait_send()
+            kf_copy(e, d).wait_send()
     for e in (1, 3):
         for d in range(1, 5):
             wy_copy(e, d).wait_send()
@@ -581,7 +601,7 @@
             dma((2, 4, 4)), dma((2, 4, 4)), dma((3,)), dma((3,)), dma((7,)), dma((7,)),
             dma((2, 3)), dma((2, 3)), dma((4,)), dma((4,)), dma((2, 4)), dma((2, 4)), dma(()), dma(()), dma((4, 4)), dma((4, 4)),
             dma((2, 3)), dma((2, 3)), dma((2,)), dma((2,)), dma((4,)), dma((4,)),
-            dma((3,)), dma((3,)), dma((3,)), dma((3,)), dma((3, 4)), dma((3, 4)), dma((4,)), dma((4,)),
+            dma((3,)), dma((3,)), dma((3,)), dma((3,)), dma((2, 4)), dma((2, 4)), dma((2, 4)), dma((2, 4)), dma((4,)), dma((4,)),
             dma((4, 3)), dma((4, 3)), dma((2, 2)), dma((2, 2)), dma((2,)), dma((2,)), dma((2, 4, 4, 2)), dma((2, 4, 4, 2)),
         ],
         compiler_params=pltpu.CompilerParams(collective_id=0, has_side_effects=True, vmem_limit_bytes=60 << 20),

time: 103 us -> 99 us (0.961)
  Pallas kernels: 100 us -> 95.7 us
    pallas_call x1, Pallas kernels: 100 us -> 95.7 us  [local(): pl.pallas_call(kernel, out_shape=jax.ShapeDtypeStruct((512, 256), BF16),...]
where the time goes in v3:
time: 99 us; the launch traced here: 97.4 us
  Pallas kernels  95.7 us (97%)
  local copies, waits for them, and re-layouts  1.67 us (2%)
    pallas_call x1, Pallas kernels, local(): pl.pallas_call(kernel, out_shape=jax.ShapeDtypeStruct((512, 256), BF16),...  95.7 us

profile of v3, /device:TPU:8, one launch (start us, length us, event | category | flops | bytes accessed | tf_op | source)
XLA Modules:
  0.0 97.4 jit_solution(9790877596774416197)
XLA Ops:
  0.0 95.7 %tree_attention.1 = bf16[512,256]{1,0:T(8,128)(2,1)} custom-call(s32[5,32]{1,0:T(8,128)} %bitcast.7, f32[64,128]{1,0:T(8,128)} %bitcast.6, bf16[512,256]{1,0:T(8,128)(2,1)} %tok.1, bf16[8,4,256,256]{3,2,1,0:T(8,128)(2,1)} %bitcast.4, bf16[64,8192]{1,0:T(8,128)(2,1)} %bitcast.5, bf16[256,8192]{1,0:T(8,128)(2,1)} %wo.1), custom_call_target="tpu_custom_call" | custom-call | flops 6000000000 | bytes 10485760 | tf_op jit(solution)/shard_map/tree_attention/pallas_call | solution.py:576
  95.7 1.7 %copy.8 = bf16[512,256]{1,0:T(8,128)(2,1)} copy(bf16[512,256]{1,0:T(8,128)(2,1)} %tree_attention.1) | data formatting | bytes 524288

commit v4 on v3

--- a/solution.py
+++ b/solution.py
@@ -94,7 +94,7 @@
     def x_used(way, hop, b):
         return hop < 3 or (b < 2) == (way == 0)
 
-    for b in range(4):
+    for b in range(2):
         for way in range(2):
             x_copy(way, 0, b).start()
 
@@ -110,8 +110,6 @@
     def p_self(x2):
         return jnp.logical_and(pair_z == z, x == x2)
 
-    for d in (1, 3, 2):
-        w_copy(0, d).start()
     for x2 in range(NX):
         cp, src, dst = p_copy(x2)
 
@@ -122,6 +120,12 @@
         @pl.when(jnp.logical_not(p_self(x2)))
         def _():
             cp.start()
+
+    for d in (1, 3, 2):
+        w_copy(0, d).start()
+    for b in range(2, 4):
+        for way in range(2):
+            x_copy(way, 0, b).start()
 
     own_x.wait()
     row_id = lax.broadcasted_iota(jnp.int32, (8, BLK), 0)
@@ -194,8 +198,7 @@
     for d in (1, 3, 2):
         w_copy(1, d).start()
     x_forward(0, (2, 3))
-    w_arrive(0, 2)
-    w_pass(2)
+
     def wo_block(strip, x2):
         return wo.at[:, pl.ds(pl.multiple_of((strip * NX + x2) * 256, 256), 256)]
 
@@ -229,12 +232,15 @@
             ref = wob.at[d, strip]
             remote(ref, ref, o_s.at[i, d - 1], o_r.at[i, d - 1], at_x(d)).wait_recv()
 
-    x_forward(1)
+    x_forward(1, (0, 1))
     for q in range(4):
         ref = wb.at[4, s, pl.ds(q * 64, 64), :]
         remote(ref, ref, p_s.at[q], p_r.at[q], sibling).wait_recv()
     w_pass(4)
     wf_copy().start()
+    w_arrive(0, 2)
+    w_pass(2)
+    x_forward(1, (2, 3))
     for d in (1, 3, 2):
         w_arrive(1, d)
         wc_copy(2, d).start()
@@ -271,10 +277,13 @@
     normalise((z + 7) % NZ)
     normalise((z + 2) % NZ)
     normalise((z + 6) % NZ)
-    for d in (1, 3, 2, 4):
+    def wy_pass(d):
         for e in (1, 3):
             wy_arrival(e, d).wait_recv()
             wc_copy(e, d).start()
+
+    for d in (1, 3, 4):
+        wy_pass(d)
     wf_arrival().wait_recv()
     wc_copy(2, 4).start()
     normalise((z + 3) % NZ)
@@ -296,6 +305,7 @@
     for d in (1, 3, 2):
         kv_copy(d).start()
 
+    wy_pass(2)
     o_arrive(0)
     oy_copy(1).start()
     oy_copy(3).start()
@@ -333,26 +343,30 @@
         ref = kf_half(lane_strip(2), d, i)
         return remote(ref, ref, kf_s.at[i, d], kf_r.at[i, d], at_y(1))
 
-    def group(strip):
-        return kvtab.at[pl.ds(strip * NX, NX)]
-
-    def kc_copy(e):
-        ref = group(lane_strip(e))
-        return remote(ref, ref, kc_s.at[e], kc_r.at[e], sibling)
-
-    def kc_arrival(e):
-        ref = group(far_strip(e))
-        return remote(ref, ref, kc_s.at[e], kc_r.at[e], sibling)
+    def kc_copy(e, d):
+        ref = kvtab.at[lane_strip(e) * NX + (x + d) % NX]
+        return remote(ref, ref, kc_s.at[e, d], kc_r.at[e, d], sibling)
+
+    def kc_arrival(e, d):
+        ref = kvtab.at[far_strip(e) * NX + (x + d) % NX]
+        return remote(ref, ref, kc_s.at[e, d], kc_r.at[e, d], sibling)
 
     def ky_pass(d):
         for e in (1, 3):
             ky_arrival(e, d).wait_recv()
             kf_copy(e, d).start()
+            kc_copy(e, d).start()
+
+    def kf_pass(d):
+        for i in range(2):
+            kf_arrival(i, d).wait_recv()
+        kc_copy(2, d).start()
 
     for d in (1, 3, 2):
         ka_copy(d).start()
     for e in (1, 3):
         ky_copy(e, 0).start()
+    kc_copy(0, 0).start()
 
     def q_copy(xa, d):
         return remote(qs.at[xa, (x + d) % NX], qr.at[3 - d, xa], q_s.at[xa, d - 1], q_r.at[xa, 3 - d], at_x(d))
@@ -376,25 +390,24 @@
         ka_arrival(d).wait_recv()
         for e in (1, 3):
             ky_copy(e, d).start()
+        kc_copy(0, d).start()
     ky_pass(0)
     ka_arrival(2).wait_recv()
     for e in (1, 3):
         ky_copy(e, 2).start()
-    kc_copy(0).start()
+    kc_copy(0, 2).start()
     for d in (1, 3):
         ky_pass(d)
+    kf_pass(0)
+    ky_pass(2)
+    for d in (1, 3):
+        kf_pass(d)
     o_arrive(1)
     oc_copy(2).start()
+    kf_pass(2)
     for e in (1, 3):
         oy_arrival(e).wait_recv()
         oc_copy(e).start()
-    ky_pass(2)
-    kc_copy(1).start()
-    kc_copy(3).start()
-    for d in (0, 1, 3, 2):
-        for i in range(2):
-            kf_arrival(i, d).wait_recv()
-    kc_copy(2).start()
 
     for xa in range(NX):
         for d in (1, 2, 3):
@@ -403,7 +416,8 @@
         qb[xa] = v.astype(BF16)
 
     for e in range(4):
-        kc_arrival(e).wait_recv()
+        for d in range(4):
+            kc_arrival(e, d).wait_recv()
 
     listed = [anc[j, block] for j in range(5)]
     tables = [kvtab[jnp.maximum(i, 0)] for i in listed] + [kvtab[block]]
@@ -428,7 +442,7 @@
         attb[x, xa] = jnp.concatenate([got[:BLK], got[BLK:]], axis=1)
 
     def half(b, h):
-        return attb.at[b, pl.ds(2 * h, 2)]
+        return attb.at[b, :, pl.ds(64 * h, 64)]
 
     def at_copy(d, h):
         return remote(half(x, h), half(x, h), at_s.at[d // 2, h], at_r.at[(3 - d) // 2, h], at_x(d))
@@ -454,24 +468,20 @@
     for e in range(4):
         oc_arrival(e).wait_recv()
 
-    def at_ready(d):
-        if d == 1:
-            at_arrival(3, 0).wait_recv()
-            af_copy(1).start()
-            at_arrival(1, 1).wait_recv()
-            af_copy(3).start()
-            at_arrival(1, 0).wait_recv()
-        elif d == 3:
-            at_arrival(3, 1).wait_recv()
+    def at_ready(d, h):
+        if d in (1, 3):
+            at_arrival(d, h).wait_recv()
+            if (d, h) in ((3, 0), (1, 1)):
+                af_copy(4 - d).start()
         elif d == 2:
-            af_arrival(0).wait_recv()
-            af_arrival(1).wait_recv()
-
-    def term(d, shard):
+            af_arrival(h).wait_recv()
+
+    def term(d, h, shard):
         b = (x + d) % NX
-        a = jnp.dot(attb[b, x], wob[0, shard], preferred_element_type=F32)
+        at = slice(h * 64, h * 64 + 64)
+        a = jnp.dot(attb[b, x, at], wob[0, shard], preferred_element_type=F32)
         for e in range(1, NX):
-            a = a + jnp.dot(attb[b, (x + e) % NX], wob[e, shard], preferred_element_type=F32)
+            a = a + jnp.dot(attb[b, (x + e) % NX, at], wob[e, shard], preferred_element_type=F32)
         return a
 
     def r_copy(way, k, d, h):
@@ -483,47 +493,40 @@
         )
 
     long_way = {0: 0, 1: 1, 3: 0, 2: 1}
-
-    def r_step(way, k, d, longest):
-        step = 1 if way == 0 else -1
-        v = term(d, (z + step * k + NZ) % NZ)
-        for h in range(2):
-            at = slice(h * 64, h * 64 + 64)
-            u = v[at]
-            if k < longest:
+    schedule = (
+        (0, 0, 0, 4), (0, 1, 0, 4), (0, 0, 1, 3), (0, 1, 1, 3), (0, 0, 0, 3), (0, 0, 1, 2), (0, 1, 0, 3),
+        (0, 1, 1, 2), (3, 0, 0, 4), (1, 1, 1, 4), (3, 0, 1, 3), (1, 1, 0, 3), (0, 0, 0, 2), (0, 0, 1, 1),
+        (0, 1, 0, 2), (0, 1, 1, 1), (3, 1, 0, 4), (1, 0, 1, 4), (3, 1, 1, 3), (1, 0, 0, 3), (3, 0, 0, 3),
+        (1, 1, 1, 3), (1, 1, 0, 2), (3, 0, 1, 2), (0, 0, 0, 1), (0, 1, 0, 1), (2, 0, 1, 4), (2, 1, 1, 4),
+        (2, 0, 0, 3), (2, 1, 0, 3), (3, 1, 0, 3), (1, 0, 1, 3), (1, 0, 0, 2), (3, 1, 1, 2), (3, 0, 0, 2),
+        (1, 1, 1, 2), (1, 1, 0, 1), (3, 0, 1, 1), (0, 0, -1, 0), (2, 0, 1, 3), (0, 1, -1, 0), (2, 1, 1, 3),
+        (2, 0, 0, 2), (1, 0, 1, 2), (2, 1, 0, 2), (3, 1, 1, 1), (3, 1, 0, 2), (1, 1, 1, 1), (1, 0, 0, 1),
+        (3, 0, 0, 1), (2, 0, 1, 2), (2, 1, 1, 2), (2, 0, 0, 1), (1, 0, 1, 1), (2, 1, 0, 1), (3, 1, 0, 1),
+        (1, 1, -1, 0), (2, 0, 1, 1), (3, 0, -1, 0), (2, 1, 1, 1), (1, 0, -1, 0), (3, 1, -1, 0), (2, 0, -1, 0),
+        (2, 1, -1, 0),
+    )
+    begun = set()
+    for d, h, way, k in schedule:
+        at = slice(h * 64, h * 64 + 64)
+        if (d, h) not in begun:
+            begun.add((d, h))
+            at_ready(d, h)
+        v = term(d, h, (z + (1 if way == 0 else -1) * k + NZ) % NZ)
+        if k == 0:
+            for one in range(2):
+                r_copy(one, 1, d, h).wait_recv()
+                v = v + rrecv[one, 0, d, at].astype(F32)
+            out[pl.ds(pl.multiple_of(((x + d) % NX) * BLK + h * 64, 64), 64), :] = v.astype(BF16)
+        else:
+            if k < (4 if way == long_way[d] else 3):
                 r_copy(way, k + 1, d, h).wait_recv()
-                u = u + rrecv[way, k, d, at].astype(F32)
-            rsend[way, k - 1, d, at] = u.astype(BF16)
+                v = v + rrecv[way, k, d, at].astype(F32)
+            rsend[way, k - 1, d, at] = v.astype(BF16)
             r_copy(way, k, d, h).start()
 
-    sent = []
-    schedule = (
-        (0, 0), (1, 0), (0, 1), (0, 3), (2, 0), (0, 2), (1, 1), (1, 3), (3, 0), (1, 2),
-        (2, 1), (2, 3), (4, 0), (2, 2), (3, 1), (3, 3), (3, 2), (4, 1), (4, 3), (4, 2),
-    )
-    for stage, d in schedule:
-        far = long_way[d]
-        if stage == 0:
-            at_ready(d)
-        if stage < 4:
-            r_step(far, 4 - stage, d, 4)
-            sent.append((far, 4 - stage, d))
-        if stage < 3:
-            r_step(1 - far, 3 - stage, d, 3)
-            sent.append((1 - far, 3 - stage, d))
-        if stage == 4:
-            v = term(d, z)
-            for h in range(2):
-                at = slice(h * 64, h * 64 + 64)
-                u = v[at]
-                for way in range(2):
-                    r_copy(way, 1, d, h).wait_recv()
-                    u = u + rrecv[way, 0, d, at].astype(F32)
-                out[pl.ds(pl.multiple_of(((x + d) % NX) * BLK + h * 64, 64), 64), :] = u.astype(BF16)
-
-    for way, k, d in sent:
-        r_copy(way, k, d, 0).wait_send()
-        r_copy(way, k, d, 1).wait_send()
+    for d, h, way, k in schedule:
+        if k > 0:
+            r_copy(way, k, d, h).wait_send()
     for b in range(4):
         for way in range(2):
             for hop in range(4):
@@ -565,7 +568,8 @@
         for d in range(1, 5):
             wc_copy(e, d).wait_send()
         oc_copy(e).wait_send()
-        kc_copy(e).wait_send()
+        for d in range(4):
+            kc_copy(e, d).wait_send()
 
 
 def local(tokens, norm_gain, query_weight, pair_weight, ancestors, out_weight):
@@ -601,7 +605,7 @@
             dma((2, 4, 4)), dma((2, 4, 4)), dma((3,)), dma((3,)), dma((7,)), dma((7,)),
             dma((2, 3)), dma((2, 3)), dma((4,)), dma((4,)), dma((2, 4)), dma((2, 4)), dma(()), dma(()), dma((4, 4)), dma((4, 4)),
             dma((2, 3)), dma((2, 3)), dma((2,)), dma((2,)), dma((4,)), dma((4,)),
-            dma((3,)), dma((3,)), dma((3,)), dma((3,)), dma((2, 4)), dma((2, 4)), dma((2, 4)), dma((2, 4)), dma((4,)), dma((4,)),
+            dma((3,)), dma((3,)), dma((3,)), dma((3,)), dma((2, 4)), dma((2, 4)), dma((2, 4)), dma((2, 4)), dma((4, 4)), dma((4, 4)),
             dma((4, 3)), dma((4, 3)), dma((2, 2)), dma((2, 2)), dma((2,)), dma((2,)), dma((2, 4, 4, 2)), dma((2, 4, 4, 2)),
         ],
         compiler_params=pltpu.CompilerParams(collective_id=0, has_side_effects=True, vmem_limit_bytes=60 << 20),

time: 99 us -> 97.4 us (0.984); the launches traced: 97.4 us -> 96.8 us
  no operation moved by 1% of the time
where the time goes in v4:
time: 97.4 us; the launch traced here: 96.8 us
  Pallas kernels  95.1 us (98%)
  local copies, waits for them, and re-layouts  1.67 us (2%)
    pallas_call x1, Pallas kernels, local(): pl.pallas_call(kernel, out_shape=jax.ShapeDtypeStruct((512, 256), BF16),...  95.1 us

profile of v4, /device:TPU:8, one launch (start us, length us, event | category | flops | bytes accessed | tf_op | source)
XLA Modules:
  0.0 96.8 jit_solution(1965390241374046300)
XLA Ops:
  0.0 95.1 %tree_attention.1 = bf16[512,256]{1,0:T(8,128)(2,1)} custom-call(s32[5,32]{1,0:T(8,128)} %bitcast.7, f32[64,128]{1,0:T(8,128)} %bitcast.6, bf16[512,256]{1,0:T(8,128)(2,1)} %tok.1, bf16[8,4,256,256]{3,2,1,0:T(8,128)(2,1)} %bitcast.4, bf16[64,8192]{1,0:T(8,128)(2,1)} %bitcast.5, bf16[256,8192]{1,0:T(8,128)(2,1)} %wo.1), custom_call_target="tpu_custom_call" | custom-call | flops 6000000000 | bytes 10485760 | tf_op jit(solution)/shard_map/tree_attention/pallas_call | solution.py:580
  95.1 1.7 %copy.8 = bf16[512,256]{1,0:T(8,128)(2,1)} copy(bf16[512,256]{1,0:T(8,128)(2,1)} %tree_attention.1) | data formatting | bytes 524288

commit v5 on v4

--- a/solution.py
+++ b/solution.py
@@ -286,6 +286,10 @@
         wy_pass(d)
     wf_arrival().wait_recv()
     wc_copy(2, 4).start()
+    o_arrive(0)
+    oy_copy(1).start()
+    oy_copy(3).start()
+    oc_copy(0).start()
     normalise((z + 3) % NZ)
     normalise((z + 5) % NZ)
     x_forward(3)
@@ -306,10 +310,6 @@
         kv_copy(d).start()
 
     wy_pass(2)
-    o_arrive(0)
-    oy_copy(1).start()
-    oy_copy(3).start()
-    oc_copy(0).start()
 
     block = s * NX + x
     for d in (1, 3, 2):
@@ -385,6 +385,8 @@
         for d in range(1, 4):
             wc_arrival(e, d).wait_recv()
     lax.fori_loop(0, 4, q_part, 0)
+    o_arrive(1)
+    oc_copy(2).start()
 
     for d in (1, 3):
         ka_arrival(d).wait_recv()
@@ -398,16 +400,14 @@
     kc_copy(0, 2).start()
     for d in (1, 3):
         ky_pass(d)
+    for e in (1, 3):
+        oy_arrival(e).wait_recv()
+        oc_copy(e).start()
     kf_pass(0)
     ky_pass(2)
     for d in (1, 3):
         kf_pass(d)
-    o_arrive(1)
-    oc_copy(2).start()
     kf_pass(2)
-    for e in (1, 3):
-        oy_arrival(e).wait_recv()
-        oc_copy(e).start()
 
     for xa in range(NX):
         for d in (1, 2, 3):

time: 97.4 us -> 96.9 us (level)
  no operation moved by 1% of the time
where the time goes in v5:
time: 96.9 us; the launch traced here: 96.5 us
  Pallas kernels  94.9 us (98%)
  local copies, waits for them, and re-layouts  1.67 us (2%)
    pallas_call x1, Pallas kernels, local(): pl.pallas_call(kernel, out_shape=jax.ShapeDtypeStruct((512, 256), BF16),...  94.9 us

profile of v5, /device:TPU:8, one launch (start us, length us, event | category | flops | bytes accessed | tf_op | source)
XLA Modules:
  0.0 96.5 jit_solution(11835660660455024147)
XLA Ops:
  0.0 94.9 %tree_attention.1 = bf16[512,256]{1,0:T(8,128)(2,1)} custom-call(s32[5,32]{1,0:T(8,128)} %bitcast.7, f32[64,128]{1,0:T(8,128)} %bitcast.6, bf16[512,256]{1,0:T(8,128)(2,1)} %tok.1, bf16[8,4,256,256]{3,2,1,0:T(8,128)(2,1)} %bitcast.4, bf16[64,8192]{1,0:T(8,128)(2,1)} %bitcast.5, bf16[256,8192]{1,0:T(8,128)(2,1)} %wo.1), custom_call_target="tpu_custom_call" | custom-call | flops 6000000000 | bytes 10485760 | tf_op jit(solution)/shard_map/tree_attention/pallas_call | solution.py:580
  94.9 1.7 %copy.8 = bf16[512,256]{1,0:T(8,128)(2,1)} copy(bf16[512,256]{1,0:T(8,128)(2,1)} %tree_attention.1) | data formatting | bytes 524288
